TPU v7x, 512 devices: a whole 4x8x8 slice. The times are simulated.
512 devices in a mesh: gx: 32 (over x_hi, z, core), gy: 16 (over y, x_lo).
Axes of the slice: x: 4 (x_hi: 2, x_lo: 2; x = x_hi * 2 + x_lo), y: 8, z: 8, core: 2. Of those that a mesh axis runs over, the one named last changes fastest.
Arguments:
- iti: float32 [32, 16, 2, 512, 512], P('gx', 'gy'), may hold values from -3 to 3
- side: int32 [32, 16], P('gx', 'gy'), may hold values from 0 to 1, as said below
- owner: int32 [32, 16, 16], P('gx', 'gy'), may hold values from 0 to 15, each once within a row
Outputs:
- panels: float32 [32, 16, 2, 16, 24, 768], P('gx', 'gy')
Inputs may be any that keep to these rules, and one draw needn't show every extreme that they name: `side`: boxes (i, j) and (i + 16, j) are the two siblings of one parent and have different sides. `owner`: for each box the owners of its panels are all different.
All inputs are finite; a program needn't handle non-finite values.
Results may differ from a plain program's by a relative error of at most 0.0003.
Values sent between devices are 32-bit elements; how exact they have to be, the bound alone decides.
A program may use at most 64 MiB of HBM per device.

v0:
```python
import math

import jax
import jax.numpy as jnp
from jax import lax
from jax.sharding import PartitionSpec as P

SWEEPS = 15


def from_partner(x, axis, bit):
    return lax.ppermute(x, axis, [(i, i ^ 1 << bit) for i in range(lax.axis_size(axis))])


def cprod(left, right):
    highest = lax.Precision.HIGHEST
    real_real = jnp.dot(left[0], right[0], precision=highest, preferred_element_type=jnp.float32)
    imag_imag = jnp.dot(left[1], right[1], precision=highest, preferred_element_type=jnp.float32)
    real_imag = jnp.dot(left[0], right[1], precision=highest, preferred_element_type=jnp.float32)
    imag_real = jnp.dot(left[1], right[0], precision=highest, preferred_element_type=jnp.float32)
    return jnp.stack([real_real - imag_imag, real_imag + imag_real])


def series_sum(interface, start):
    total = start
    power = interface
    levels = (SWEEPS + 1).bit_length() - 1
    for level in range(levels):
        total = total + cprod(power, total)
        if level + 1 < levels:
            power = cprod(power, power)
    return total


def on_device(iti, side, owner):
    ownmap = iti[0, 0]
    edge = ownmap.shape[-1] // 4
    ext = 3 * edge
    bit_index = lax.axis_size("gx").bit_length() - 2
    partner = from_partner(ownmap[:, ext:, :], "gx", bit_index)
    p_ss = partner[:, :, ext:]
    p_se = partner[:, :, :ext]
    interface = cprod(p_ss, ownmap[:, ext:, ext:])
    own_cols = cprod(p_ss, ownmap[:, ext:, :ext])
    flag = side[0, 0] == 1
    west_start = jnp.where(flag, p_se, own_cols)
    east_start = jnp.where(flag, own_cols, p_se)
    exterior = ownmap[:, :ext, :ext]
    zero = jnp.zeros_like(exterior)
    west_base = jnp.where(flag, zero, exterior)
    east_base = jnp.where(flag, exterior, zero)
    coupling = ownmap[:, :ext, ext:]
    weight = math.sqrt(edge)
    groups = lax.axis_size("gy")
    rows_each = ext // groups
    places = jnp.arange(groups, dtype=jnp.int32)
    match = (owner[0, 0][:, None] == places[None, :]).astype(jnp.int32)
    inverse = jnp.sum(places[:, None] * match, axis=0)
    merged = (
        jnp.concatenate([west_base, east_base], axis=-1)
        + cprod(coupling, series_sum(interface, jnp.concatenate([west_start, east_start], axis=-1)))
    ) * weight
    split = merged.reshape(2, groups, rows_each, merged.shape[-1])
    sent = jnp.take(split, inverse, axis=1)
    received = lax.all_to_all(sent, "gy", split_axis=1, concat_axis=1, tiled=True)
    return received[None, None]


def solution(mesh):
    in_specs = (P("gx", "gy", None, None, None), P("gx", "gy"), P("gx", "gy", None))
    out_specs = P("gx", "gy", None, None, None, None)
    return jax.shard_map(
        on_device, mesh=mesh, in_specs=in_specs, out_specs=out_specs, check_vma=False
    )
```

profile of v0, /device:TPU:448, one launch (start us, length us, event | category | flops | bytes accessed | tf_op | source)
XLA Modules:
  0.0 105.9 jit_solution(8220964391231694844)
XLA Ops:
  0.0 1.2 %slice.121 = f32[2,128,512]{2,1,0:T(8,128)S(1)} slice(f32[2,512,512]{2,1,0:T(8,128)} %bitcast.155), slice={[0:2], [384:512], [0:512]} | slice | bytes 1048576 | tf_op jit(solution)/shard_map/slice | solution.py:40
  1.2 4.9 %collective-permute-start = (f32[2,128,512]{2,1,0:T(8,128)S(1)}, f32[2,128,512]{2,1,0:T(8,128)S(1)}, u32[]{:S(2)}, u32[]{:S(2)}) collective-permute-start(f32[2,128,512]{2,1,0:T(8,128)S(1)} %slice.121), channel_id=1, source_target_pairs={{0,256},{16,272},{32,288},{48,304},{64,320},{80,336},{96,352},{112... | collective-permute-start | bytes 1572872 | tf_op jit(solution)/shard_map/ppermute | solution.py:12
  6.8 0.7 select_reduce_fusion
  7.6 1.4 %slice_select_fusion.1 = (f32[2,384,384]{2,1,0:T(8,128)S(1)}, f32[2,384,384]{2,1,0:T(8,128)S(1)}) fusion(f32[2,512,512]{2,1,0:T(8,128)} %bitcast.156, pred[]{:T(512)} %bitcast.1), kind=kLoop, calls=%fused_computation.35 | loop fusion | flops 589824 | bytes 3538945 | tf_op jit(solution)/shard_map/jit(_where)/select_n | solution.py:50
  9.0 9.2 %collective-permute-done = f32[2,128,512]{2,1,0:T(8,128)S(1)} collective-permute-done((f32[2,128,512]{2,1,0:T(8,128)S(1)}, f32[2,128,512]{2,1,0:T(8,128)S(1)}, u32[]{:S(2)}, u32[]{:S(2)}) %collective-permute-start) | collective-permute-done | bytes 524320 | tf_op jit(solution)/shard_map/ppermute | solution.py:12
  18.3 0.3 fusion.25
  18.6 0.3 fusion.24
  18.9 0.2 fusion.27
  19.1 0.3 fusion.10
  19.5 0.3 fusion.9
  19.8 0.2 convolution_subtract_fusion.9
  20.1 0.5 fusion.32
  20.6 0.5 fusion.28
  21.0 0.2 fusion.39
  21.2 0.2 fusion.26
  21.4 0.2 convolution_add_fusion.9
  21.9 0.5 fusion.8
  22.3 0.5 fusion.7
  22.8 0.2 convolution_subtract_fusion.8
  23.2 0.5 fusion.16
  23.6 0.5 fusion.17
  24.1 0.2 fusion.41
  24.3 0.2 convolution_add_fusion.8
  24.7 0.5 fusion.6
  25.2 0.5 fusion.5
  25.7 0.2 convolution_subtract_fusion.7
  26.0 0.5 fusion.18
  26.5 0.5 fusion.19
  27.0 0.2 fusion.43
  27.2 0.2 convolution_add_fusion.7
  27.4 0.2 fusion.44
  27.6 0.5 fusion.4
  28.1 0.5 fusion.3
  28.6 0.2 convolution_subtract_fusion.6
  28.9 0.5 fusion.20
  29.4 0.5 fusion.21
  29.9 0.2 convolution_add_fusion.6
  30.1 0.5 fusion.2
  30.5 0.5 fusion.1
  31.2 1.1 %fusion.22 = f32[768,384]{0,1:T(8,128)S(1)} fusion(f32[2,128,768]{2,1,0:T(8,128)S(1)} %maximum_add_fusion.3, f32[2,512,512]{2,1,0:T(8,128)S(1)} %bitcast.165), kind=kOutput, calls=%fused_computation.64 | convolution fusion | flops 452984832 | bytes 1769472 | tf_op jit(solution)/shard_map/dot_general | solution.py:17
  32.3 1.3 %fusion.23 = f32[768,384]{0,1:T(8,128)S(1)} fusion(f32[2,128,768]{2,1,0:T(8,128)S(1)} %maximum_add_fusion.3, f32[2,512,512]{2,1,0:T(8,128)S(1)} %bitcast.166), kind=kOutput, calls=%fused_computation.65 | convolution fusion | flops 452984832 | bytes 1769472 | tf_op jit(solution)/shard_map/dot_general | solution.py:19
  33.6 1.1 %convolution_subtract_fusion = f32[768,384]{0,1:T(8,128)S(1)} fusion(f32[768,384]{0,1:T(8,128)S(1)} %fusion.22, f32[2,128,768]{2,1,0:T(8,128)S(1)} %maximum_add_fusion.3, f32[2,512,512]{2,1,0:T(8,128)S(1)} %bitcast.167), kind=kOutput, calls=%fused_computation.5 | convolution fusion | flops 453279744 | bytes 2949120 | tf_op jit(solution)/shard_map/dot_general | solution.py:18
  34.8 1.1 %convolution_add_fusion = f32[768,384]{0,1:T(8,128)S(1)} fusion(f32[768,384]{0,1:T(8,128)S(1)} %fusion.23, f32[2,128,768]{2,1,0:T(8,128)S(1)} %maximum_add_fusion.3, f32[2,512,512]{2,1,0:T(8,128)S(1)} %bitcast.168), kind=kOutput, calls=%fused_computation.4 | convolution fusion | flops 453279744 | bytes 2949120 | tf_op jit(solution)/shard_map/dot_general | solution.py:20
  35.9 0.3 fusion
  36.1 2.1 %gather_fusion = f32[16,2,24,768]{3,2,1,0:T(8,128)} fusion(f32[2,16,24,768]{3,2,1,0:T(8,128)S(1)} %fusion, s32[1024]{0:T(1024)S(1)} %pad_clamp_fusion), kind=kCustom, calls=%fused_computation | custom fusion | bytes 4718656 | tf_op jit(solution)/shard_map/jit(_take)/gather | solution.py:64
  38.2 2.0 %select_bitcast_fusion = f32[2,16,24,768]{3,2,0,1:T(8,128)S(1)} fusion(f32[16,2,24,768]{3,2,1,0:T(8,128)} %gather_fusion, pred[16]{0:T(512)(128)(4,1)S(1)} %compare_and_fusion), kind=kLoop, calls=%fused_computation.3 | loop fusion | flops 589824 | bytes 4718608 | tf_op jit(solution)/shard_map/jit(_take)/select_n | solution.py:64
  40.2 64.2 %all_to_all.5 = f32[2,16,24,768]{3,2,0,1:T(8,128)S(1)} all-to-all(f32[2,16,24,768]{3,2,0,1:T(8,128)S(1)} %select_bitcast_fusion), channel_id=1, replica_groups=mesh['gx'=32,'gy'=16] {'gy'}, dimensions={1} | all-to-all | bytes 4718592 | tf_op jit(solution)/shard_map/all_to_all | solution.py:65
  104.4 1.6 %copy.5 = f32[1,1,2,16,24,768]{5,4,3,2,1,0:T(8,128)} copy(f32[1,1,2,16,24,768]{5,4,2,3,1,0:T(8,128)S(1)} %bitcast.154) | data formatting | bytes 4718592 | tf_op jit(solution)/shard_map/broadcast_in_dim | solution.py:66
  (12 shorter events, 1.0 us)
Async XLA Ops:
  0.0 18.3 %copy-start = (f32[1,1,2,512,512]{4,3,2,1,0:T(8,128)S(1)}, f32[1,1,2,512,512]{4,3,2,1,0:T(8,128)}, u32[]{:S(2)}) copy-start(f32[1,1,2,512,512]{4,3,2,1,0:T(8,128)} %param.3) | copy-start | bytes 6291460
  1.2 17.1 %collective-permute-start = (f32[2,128,512]{2,1,0:T(8,128)S(1)}, f32[2,128,512]{2,1,0:T(8,128)S(1)}, u32[]{:S(2)}, u32[]{:S(2)}) collective-permute-start(f32[2,128,512]{2,1,0:T(8,128)S(1)} %slice.121), channel_id=1, source_target_pairs={{0,256},{16,272},{32,288},{48,304},{64,320},{80,336},{96,352},{112... | collective-permute-start | bytes 1572872 | tf_op jit(solution)/shard_map/ppermute | solution.py:12
where the time goes:
time: 106 us
  blocking collectives  64.2 us (61%)
  matrix products  16.6 us (16%)
  waiting for transfers between devices  9.24 us (9%)
  other arithmetic  5.02 us (5%)
  starting transfers between devices  4.93 us (5%)
  local copies, waits for them, and re-layouts  4.9 us (5%)
    all_to_all x1, blocking collectives, on_device(): lax.all_to_all(sent, 'gy', split_axis=1, concat_axis=1, tiled=True)  64.2 us
    ppermute x1, waiting for transfers between devices, from_partner(): lax.ppermute(x, axis, [(i, i ^ 1 << bit) for i in range(lax.axis_size(axi...  9.24 us
    ppermute x1, starting transfers between devices, from_partner(): lax.ppermute(x, axis, [(i, i ^ 1 << bit) for i in range(lax.axis_size(axi...  4.93 us
    dot_general x10, matrix products, cprod(): jnp.dot(left[0], right[1], precision=highest, preferred_element_type=jnp....  4.3 us
    dot_general x10, matrix products, cprod(): jnp.dot(left[1], right[0], precision=highest, preferred_element_type=jnp....  4.12 us
    dot_general x10, matrix products, cprod(): jnp.dot(left[1], right[1], precision=highest, preferred_element_type=jnp....  4.12 us
    dot_general x10, matrix products, cprod(): jnp.dot(left[0], right[0], precision=highest, preferred_element_type=jnp....  4.09 us
  transfers between devices with their start and end apart: 1, of which 1 were waited for; matrix products, arithmetic and copies ran while one was open for 2% of the time, Pallas kernels for 0%

commit v1 on v0

v1 whole, which is shorter than its diff:
```python
import functools
import math

import jax
import jax.numpy as jnp
from jax import lax
from jax.experimental import pallas as pl
from jax.experimental.pallas import tpu as pltpu
from jax.sharding import PartitionSpec as P

SWEEPS = 15
MESH = pl.DeviceIdType.MESH
f32, bf16 = jnp.float32, jnp.bfloat16


def split(x):
    high = x.astype(bf16)
    return high, (x - high.astype(f32)).astype(bf16)


def right_form(x):
    n = x.shape[1] // 2
    return jnp.concatenate([x, jnp.concatenate([-x[:, n:], x[:, :n]], axis=1)], axis=0)


def product(left, right):
    dot = functools.partial(jnp.dot, preferred_element_type=f32)
    return dot(left[0], right[0]) + (dot(left[0], right[1]) + dot(left[1], right[0]))


def both(x):
    high, low = split(x)
    return right_form(high), right_form(low)


def kernel(
    gx_size, ring, near,
    owner, side, iti, own_out, other_out, flag_out,
    box, qss, qse, left, left_high, left_low, own_send, other_send, flag_send, powers_high, powers_low, start,
    load_sem, edge_send, edge_recv, own_ssem, own_rsem, other_ssem, other_rsem, flag_ssem, flag_rsem, local_sem,
):
    edge = box.shape[-1] // 4
    ext = 3 * edge
    groups = ring * near
    rows = ext // groups
    weight = math.sqrt(edge)
    gx, gy = lax.axis_index("gx"), lax.axis_index("gy")
    y, x = gy // near, lax.rem(gy, near)
    sibling = (lax.rem(gx + gx_size // 2, gx_size), gy)
    half = ring // 2
    steps = [half]
    for s in range(half - 1, 0, -1):
        steps += [s, ring - s]
    places = [(s, t) for s in steps for t in range(near)] + [(0, t) for t in range(1, near)]
    peers = [lax.rem(y + s, ring) * near + lax.rem(x + t, near) for s, t in places]
    blocks = peers + [gy]
    n_peers = len(peers)

    loads = [
        pltpu.make_async_copy(iti.at[0, 0, :, ext:, :], box.at[:, ext:, :], load_sem.at[0]),
        pltpu.make_async_copy(iti.at[0, 0, :, :ext, :], box.at[:, :ext, :], load_sem.at[1]),
    ]
    for load in loads:
        load.start()
    barrier = pltpu.get_barrier_semaphore()
    pl.semaphore_signal(barrier, inc=1, device_id=sibling, device_id_type=MESH)
    for peer in peers:
        pl.semaphore_signal(barrier, inc=1, device_id=(gx, peer), device_id_type=MESH)
    flag_send[...] = jnp.full(flag_send.shape, side[0, 0].astype(f32))
    pl.semaphore_wait(barrier, n_peers + 1)

    ss = pltpu.make_async_remote_copy(
        iti.at[0, 0, :, ext:, ext:], qss, edge_send.at[0], edge_recv.at[0], device_id=sibling, device_id_type=MESH
    )
    se = pltpu.make_async_remote_copy(
        iti.at[0, 0, :, ext:, :ext], qse, edge_send.at[1], edge_recv.at[1], device_id=sibling, device_id_type=MESH
    )
    ss.start()
    se.start()
    flags = [
        pltpu.make_async_remote_copy(
            flag_send, flag_out.at[gy], flag_ssem.at[k], flag_rsem.at[k], device_id=(gx, peer), device_id_type=MESH
        )
        for k, peer in enumerate(peers)
    ]
    for flag in flags:
        flag.start()
    own_flag = pltpu.make_async_copy(flag_send, flag_out.at[gy], local_sem.at[0])
    own_flag.start()

    at = []
    for block in blocks:
        panel = jnp.int32(0)
        for p in range(groups):
            panel = jnp.maximum(panel, (owner[0, 0, p] == block).astype(jnp.int32) * p)
        at.append(panel * rows)
    for load in loads:
        load.wait()
    for k in range(groups):
        for c in range(2):
            left[k * rows:(k + 1) * rows, c * edge:(c + 1) * edge] = box[c, pl.ds(at[k], rows), ext:]
    high, low = split(left[...])
    left_high[...] = high
    left_low[...] = low
    edge_rows = [box[c, ext:, :] for c in range(2)]
    rss = both(jnp.concatenate([r[:, ext:] for r in edge_rows], axis=1))
    rse = both(jnp.concatenate([r[:, :ext] for r in edge_rows], axis=1))

    ss.wait_recv()
    q = split(jnp.concatenate([qss[0], qss[1]], axis=1))
    power = product(q, rss)
    total = product(q, rse)
    levels = (SWEEPS + 1).bit_length() - 1
    for level in range(levels):
        high, low = split(power)
        powers_high[level] = high
        powers_low[level] = low
        total = total + product((high, low), both(total))
        if level + 1 < levels:
            power = product((high, low), (right_form(high), right_form(low)))

    def send(total, base, buffer, out, ssem, rsem):
        factor = both(total)
        copies = []
        step = 4
        for g in range(0, groups, step):
            at_rows = slice(g * rows, (g + step) * rows)
            part = product((left_high[at_rows], left_low[at_rows]), factor)
            for k in range(g, g + step):
                for c in range(2):
                    piece = part[(k - g) * rows:(k - g + 1) * rows, c * ext:(c + 1) * ext]
                    if base:
                        piece = box[c, pl.ds(at[k], rows), :ext] + piece
                    buffer[k, c] = piece * weight
                if k < n_peers:
                    copy = pltpu.make_async_remote_copy(
                        buffer.at[k], out.at[:, gy], ssem.at[k], rsem.at[k],
                        device_id=(gx, peers[k]), device_id_type=MESH,
                    )
                else:
                    copy = pltpu.make_async_copy(buffer.at[k], out.at[:, gy], ssem.at[k])
                copy.start()
                copies.append(copy)
        return copies

    copies = send(total, True, own_send, own_out, own_ssem, own_rsem)
    se.wait_recv()
    total = jnp.concatenate([qse[0], qse[1]], axis=1)
    for level in range(levels):
        total = total + product((powers_high[level], powers_low[level]), both(total))
    copies += send(total, False, other_send, other_out, other_ssem, other_rsem)
    ss.wait_send()
    se.wait_send()
    own_flag.wait()
    for flag in flags:
        flag.wait()
    for copy in copies:
        copy.wait()


def on_device(ring, near, iti, side, owner):
    width = iti.shape[-1]
    edge = width // 4
    ext = 3 * edge
    groups = ring * near
    rows = ext // groups
    levels = (SWEEPS + 1).bit_length() - 1
    part = jax.ShapeDtypeStruct((2, groups, rows, ext), f32)
    dma = pltpu.SemaphoreType.DMA
    smem = pl.BlockSpec(memory_space=pltpu.SMEM)
    hbm = pl.BlockSpec(memory_space=pl.ANY)
    pinned = pl.BlockSpec(memory_space=pltpu.HBM)
    own, other, flags = pl.pallas_call(
        functools.partial(kernel, lax.axis_size("gx"), ring, near),
        out_shape=[part, part, jax.ShapeDtypeStruct((groups, 8, 128), f32)],
        in_specs=[smem, smem, pinned],
        out_specs=[hbm, hbm, hbm],
        scratch_shapes=[
            pltpu.VMEM((2, width, width), f32),
            pltpu.VMEM((2, edge, edge), f32),
            pltpu.VMEM((2, edge, ext), f32),
            pltpu.VMEM((ext, 2 * edge), f32),
            pltpu.VMEM((ext, 2 * edge), bf16),
            pltpu.VMEM((ext, 2 * edge), bf16),
            pltpu.VMEM((groups, 2, rows, ext), f32),
            pltpu.VMEM((groups, 2, rows, ext), f32),
            pltpu.VMEM((8, 128), f32),
            pltpu.VMEM((levels, edge, 2 * edge), bf16),
            pltpu.VMEM((levels, edge, 2 * edge), bf16),
            pltpu.VMEM((edge, 2 * ext), f32),
            dma((2,)), dma((2,)), dma((2,)),
            dma((groups,)), dma((groups,)), dma((groups,)), dma((groups,)), dma((groups,)), dma((groups,)),
            dma((1,)),
        ],
        compiler_params=pltpu.CompilerParams(
            collective_id=0, has_side_effects=True, vmem_limit_bytes=48 * 2**20
        ),
        name="merge",
    )(owner, side, iti)
    east = flags[:, 0, 0][None, :, None, None] == 1
    west_half = jnp.where(east, other, own)
    east_half = jnp.where(east, own, other)
    return jnp.concatenate([west_half, east_half], axis=-1)[None, None]


def solution(mesh):
    in_specs = (P("gx", "gy", None, None, None), P("gx", "gy"), P("gx", "gy", None))
    out_specs = P("gx", "gy", None, None, None, None)
    near = 2
    body = functools.partial(on_device, mesh.shape["gy"] // near, near)
    return jax.shard_map(body, mesh=mesh, in_specs=in_specs, out_specs=out_specs, check_vma=False)
```

time: 106 us -> 74.8 us (0.71)
  Pallas kernels: 0 us -> 69.1 us
  blocking collectives: 64.2 us -> 0 us
  matrix products: 16.6 us -> 0 us
  waiting for transfers between devices: 9.24 us -> 0 us
  starting transfers between devices: 4.93 us -> 0 us
  other arithmetic: 5.02 us -> 2.21 us
  local copies, waits for them, and re-layouts: 4.9 us -> 2.24 us
    pallas_call x0 -> x1, Pallas kernels: none -> 69.1 us  [on_device(): pl.pallas_call(functools.partial(kernel, lax.axis_size('gx'), ring, near)...]
    all_to_all x1 -> x0, blocking collectives: 64.2 us -> none  [on_device(): lax.all_to_all(sent, 'gy', split_axis=1, concat_axis=1, tiled=True)]
    dot_general x40 -> x0, matrix products: 16.6 us -> none  [the longest x10 4.3 us: cprod(): jnp.dot(left[0], right[1], precision=highest, preferred_element_type=jnp....]
    ppermute x1 -> x0, waiting for transfers between devices: 9.24 us -> none  [from_partner(): lax.ppermute(x, axis, [(i, i ^ 1 << bit) for i in range(lax.axis_size(axi...]
    ppermute x1 -> x0, starting transfers between devices: 4.93 us -> none  [from_partner(): lax.ppermute(x, axis, [(i, i ^ 1 << bit) for i in range(lax.axis_size(axi...]
    select_n x4 -> x1, other arithmetic: 3.48 us -> 0.24 us  [on_device(): west_half = jnp.where(east, other, own)]
    unnamed x2 -> x4, local copies, waits for them, and re-layouts: 0.01 us -> 2.24 us
    gather x1 -> x0, local copies, waits for them, and re-layouts: 2.1 us -> none  [on_device(): sent = jnp.take(split, inverse, axis=1)]
  transfers between devices with their start and end apart: 1 -> 0, of which waited for: 1 -> 0; matrix products, arithmetic and copies ran while one was open for 2% -> 0% of each run, Pallas kernels for 0% -> 0%
where the time goes in v1:
time: 74.8 us; the launch traced here: 74.3 us
  Pallas kernels  69.1 us (92%)
  local copies, waits for them, and re-layouts  2.24 us (3%)
  other arithmetic  2.21 us (3%)
    pallas_call x1, Pallas kernels, on_device(): pl.pallas_call(functools.partial(kernel, lax.axis_size('gx'), ring, near)...  69.1 us
    unnamed x4, local copies, waits for them, and re-layouts  2.24 us
    broadcast_in_dim x1, other arithmetic, on_device(): return jnp.concatenate([west_half, east_half], axis=-1)[None, None]  1.6 us

profile of v1, /device:TPU:448, one launch (start us, length us, event | category | flops | bytes accessed | tf_op | source)
XLA Modules:
  0.0 74.3 jit_solution(3311384088512047593)
XLA Ops:
  0.7 0.0 copy-start
  0.7 1.6 %copy-done = f32[1,1,2,512,512]{4,3,2,1,0:T(8,128)S(1)} copy-done((f32[1,1,2,512,512]{4,3,2,1,0:T(8,128)S(1)}, f32[1,1,2,512,512]{4,3,2,1,0:T(8,128)}, u32[]{:S(2)}) %copy-start) | copy-done | bytes 2097176
  2.2 0.0 copy-start.1
  2.2 0.7 copy-done.1
  2.9 69.1 %merge.1 = (f32[2,16,24,384]{3,2,1,0:T(8,128)S(1)}, f32[2,16,24,384]{3,2,1,0:T(8,128)S(1)}, f32[16,8,128]{2,1,0:T(8,128)S(1)}) custom-call(s32[1,1,16]{2,1,0:T(1,128)S(1)} %copy-done.1, s32[1,1]{1,0:T(1,128)S(6)} %copy.4.side, f32[1,1,2,512,512]{4,3,2,1,0:T(8,128)S(1)} %copy-done), custom_call_target="tpu_custom_call" | custom-call | tf_op jit(solution)/shard_map/merge/pallas_call | solution.py:173
  72.1 0.4 compare_reduce_fusion
  72.4 0.2 broadcast_select_fusion.1
  72.7 1.6 %maximum_bitcast_fusion = f32[1,1,2,16,24,768]{5,4,3,2,1,0:T(8,128)} fusion(f32[2,16,24,384]{3,2,1,0:T(8,128)S(1)} %get-tuple-element.12, f32[2,16,24,384]{3,2,1,0:T(8,128)S(1)} %get-tuple-element.11), kind=kLoop, calls=%fused_computation | loop fusion | flops 589824 | bytes 4718592 | tf_op jit(solution)/shard_map/broadcast_in_dim | solution.py:203
Async XLA Ops:
  0.7 1.6 %copy-start = (f32[1,1,2,512,512]{4,3,2,1,0:T(8,128)S(1)}, f32[1,1,2,512,512]{4,3,2,1,0:T(8,128)}, u32[]{:S(2)}) copy-start(f32[1,1,2,512,512]{4,3,2,1,0:T(8,128)} %iti.1) | copy-start | bytes 6291460
  2.2 0.7 copy-start.1

commit v2 on v0

v2 whole, which is shorter than its diff:
```python
import functools
import math

import jax
import jax.numpy as jnp
from jax import lax
from jax.experimental import pallas as pl
from jax.experimental.pallas import tpu as pltpu
from jax.sharding import PartitionSpec as P

SWEEPS = 15
LEVELS = (SWEEPS + 1).bit_length() - 1
MESH = pl.DeviceIdType.MESH
f32, bf16 = jnp.float32, jnp.bfloat16
VMEM, HBM, SMEM = (pl.BlockSpec(memory_space=m) for m in (pltpu.VMEM, pltpu.HBM, pltpu.SMEM))
ANY = pl.BlockSpec(memory_space=pl.ANY)
DMA = pltpu.SemaphoreType.DMA


def split(x):
    high = x.astype(bf16)
    return high, (x - high.astype(f32)).astype(bf16)


def right_form(x):
    n = x.shape[1] // 2
    return jnp.concatenate([x, jnp.concatenate([-x[:, n:], x[:, :n]], axis=1)], axis=0)


def product(left, right):
    dot = functools.partial(jnp.dot, preferred_element_type=f32)
    return dot(left[0], right[0]) + (dot(left[0], right[1]) + dot(left[1], right[0]))


def both(x):
    high, low = split(x)
    return right_form(high), right_form(low)


def layout(ring, near):
    gy = lax.axis_index("gy")
    y, x = gy // near, lax.rem(gy, near)
    steps = [0]
    for s in range(1, ring // 2):
        steps += [s, ring - s]
    steps.append(ring // 2)
    places = [(s, t) for s in steps for t in range(near) if s or t]
    peers = [lax.rem(y + s, ring) * near + lax.rem(x + t, near) for s, t in places]
    senders = [lax.rem(y + ring - s, ring) * near + lax.rem(x + near - t, near) for s, t in places]
    return gy, peers, senders


def sibling_of(gx_size):
    return lax.rem(lax.axis_index("gx") + gx_size // 2, gx_size), lax.axis_index("gy")


def prepare(
    gx_size, ring, near,
    owner, side, iti,
    qss, edge_high, edge_low, ext_high, ext_low, left_high, left_low, base, flag,
    owner_s, box, left, load_sem, send_sem, recv_sem,
):
    edge = qss.shape[-1]
    ext = 3 * edge
    groups = ring * near
    rows = ext // groups
    loads = [
        pltpu.make_async_copy(owner, owner_s, load_sem.at[0]),
        pltpu.make_async_copy(iti.at[0, 0, :, ext:, :], box.at[:, ext:, :], load_sem.at[1]),
        pltpu.make_async_copy(iti.at[0, 0, :, :ext, :], box.at[:, :ext, :], load_sem.at[2]),
    ]
    sibling = sibling_of(gx_size)
    barrier = pltpu.get_barrier_semaphore()
    pl.semaphore_signal(barrier, inc=1, device_id=sibling, device_id_type=MESH)
    for load in loads:
        load.start()
    pl.semaphore_wait(barrier, 1)
    copy = pltpu.make_async_remote_copy(
        iti.at[0, 0, :, ext:, ext:], qss, send_sem, recv_sem, device_id=sibling, device_id_type=MESH
    )
    copy.start()

    for load in loads:
        load.wait()
    edge_rows = [box[c, ext:, :] for c in range(2)]
    edge_high[...], edge_low[...] = both(jnp.concatenate([r[:, ext:] for r in edge_rows], axis=1))
    ext_high[...], ext_low[...] = both(jnp.concatenate([r[:, :ext] for r in edge_rows], axis=1))
    flag[...] = jnp.full(flag.shape, side[0, 0].astype(f32))
    gy, peers, _ = layout(ring, near)
    owners = [owner_s[0, 0, p] for p in range(groups)]
    for k, block in enumerate(peers + [gy]):
        panel = jnp.int32(0)
        for p in range(1, groups):
            panel = jnp.maximum(panel, (owners[p] == block).astype(jnp.int32) * p)
        for c in range(2):
            found = box[c, pl.ds(panel * rows, rows), :]
            left[k * rows:(k + 1) * rows, c * edge:(c + 1) * edge] = found[:, ext:]
            base[k, c] = found[:, :ext] * math.sqrt(edge)
    left_high[...], left_low[...] = split(left[...])
    copy.wait()


def merge(
    gx_size, ring, near,
    iti, qss, edge_high, edge_low, ext_high, ext_low, left_high, left_low, base, flag,
    out,
    qse, own_send, other_send, own_in, other_in, flag_in, powers_high, powers_low,
    edge_ssem, edge_rsem, own_ssem, own_rsem, other_ssem, other_rsem, flag_ssem, flag_rsem,
):
    edge = qss.shape[-1]
    ext = 3 * edge
    groups = ring * near
    rows = ext // groups
    weight = math.sqrt(edge)
    gx = lax.axis_index("gx")
    gy, peers, senders = layout(ring, near)
    sibling = sibling_of(gx_size)
    n_peers = len(peers)

    barrier = pltpu.get_barrier_semaphore()
    for peer in reversed(peers):
        pl.semaphore_signal(barrier, inc=1, device_id=(gx, peer), device_id_type=MESH)
    pl.semaphore_signal(barrier, inc=1, device_id=sibling, device_id_type=MESH)

    q = split(jnp.concatenate([qss[0], qss[1]], axis=1))
    power = product(q, (edge_high[...], edge_low[...]))
    total = product(q, (ext_high[...], ext_low[...]))
    for level in range(LEVELS):
        high, low = split(power)
        powers_high[level] = high
        powers_low[level] = low
        total = total + product((high, low), both(total))
        if level + 1 < LEVELS:
            power = product((high, low), (right_form(high), right_form(low)))

    step = 4

    def compute(total, add, buffer):
        factor = both(total)

        def part(g):
            at_rows = slice(g * rows, (g + step) * rows)
            value = product((left_high[at_rows], left_low[at_rows]), factor) * weight
            for k in range(g, g + step):
                for c in range(2):
                    piece = value[(k - g) * rows:(k - g + 1) * rows, c * ext:(c + 1) * ext]
                    buffer[k, c] = base[k, c] + piece if add else piece

        return part

    def send(g, buffer, into, ssem, rsem):
        copies = []
        for k in range(g, min(g + step, n_peers)):
            copy = pltpu.make_async_remote_copy(
                buffer.at[k], into.at[k], ssem.at[k], rsem.at[k], device_id=(gx, peers[k]), device_id_type=MESH
            )
            copy.start()
            copies.append(copy)
        return copies

    own = compute(total, True, own_send)
    own(0)
    pl.semaphore_wait(barrier, n_peers + 1)
    own_copies = send(0, own_send, own_in, own_ssem, own_rsem)
    se = pltpu.make_async_remote_copy(
        iti.at[0, 0, :, ext:, :ext], qse, edge_ssem, edge_rsem, device_id=sibling, device_id_type=MESH
    )
    se.start()
    for g in range(step, groups, step):
        own(g)
        own_copies += send(g, own_send, own_in, own_ssem, own_rsem)
    flags = [
        pltpu.make_async_remote_copy(
            flag, flag_in.at[k], flag_ssem.at[k], flag_rsem.at[k], device_id=(gx, peer), device_id_type=MESH
        )
        for k, peer in enumerate(peers)
    ]
    for copy in flags:
        copy.start()
    se.wait()
    total = jnp.concatenate([qse[0], qse[1]], axis=1)
    for level in range(LEVELS):
        total = total + product((powers_high[level], powers_low[level]), both(total))
    other = compute(total, False, other_send)
    other_copies = []
    for g in range(0, groups, step):
        other(g)
        other_copies += send(g, other_send, other_in, other_ssem, other_rsem)

    def arrange(own_part, other_part, east, sender):
        for c in range(2):
            east_rows = jnp.broadcast_to(east[:1, :1], (rows, ext)) == 1
            a, b = own_part[c], other_part[c]
            out[c, sender, :, :ext] = jnp.where(east_rows, b, a)
            out[c, sender, :, ext:] = jnp.where(east_rows, a, b)

    arrange(own_send.at[n_peers], other_send.at[n_peers], flag[...], gy)
    for k in range(n_peers):
        flags[k].wait()
        own_copies[k].wait()
        other_copies[k].wait()
        arrange(own_in.at[k], other_in.at[k], flag_in[k], senders[k])


def write(arranged, out, sem):
    parts, groups = arranged.shape[:2]
    copies = [
        pltpu.make_async_copy(arranged.at[c, g], out.at[0, 0, c, g], sem.at[c, g])
        for c in range(parts) for g in range(groups)
    ]
    for copy in copies:
        copy.start()
    for copy in copies:
        copy.wait()


def on_device(gx_size, ring, near, iti, side, owner):
    width = iti.shape[-1]
    edge = width // 4
    ext = 3 * edge
    groups = ring * near
    rows = ext // groups
    shape = jax.ShapeDtypeStruct
    params = functools.partial(pltpu.CompilerParams, has_side_effects=True, vmem_limit_bytes=40 * 2**20)
    iti, owner = (pltpu.with_memory_space_constraint(a, pltpu.HBM) for a in (iti, owner))
    prepared = pl.pallas_call(
        functools.partial(prepare, gx_size, ring, near),
        out_shape=[
            shape((2, edge, edge), f32),
            shape((2 * edge, 2 * edge), bf16), shape((2 * edge, 2 * edge), bf16),
            shape((2 * edge, 2 * ext), bf16), shape((2 * edge, 2 * ext), bf16),
            shape((ext, 2 * edge), bf16), shape((ext, 2 * edge), bf16),
            shape((groups, 2, rows, ext), f32),
            shape((1, 128), f32),
        ],
        in_specs=[HBM, SMEM, HBM],
        out_specs=[VMEM] * 9,
        scratch_shapes=[
            pltpu.SMEM((1, 1, groups), jnp.int32),
            pltpu.VMEM((2, width, width), f32), pltpu.VMEM((ext, 2 * edge), f32),
            DMA((3,)), DMA, DMA,
        ],
        compiler_params=params(collective_id=0),
        name="prepare",
    )(owner, side, iti)
    arranged = pl.pallas_call(
        functools.partial(merge, gx_size, ring, near),
        out_shape=shape((2, groups, rows, 2 * ext), f32),
        in_specs=[HBM] + [VMEM] * 9,
        out_specs=VMEM,
        scratch_shapes=[
            pltpu.VMEM((2, edge, ext), f32),
            *[pltpu.VMEM((groups, 2, rows, ext), f32)] * 4,
            pltpu.VMEM((groups, 1, 128), f32),
            *[pltpu.VMEM((LEVELS, edge, 2 * edge), bf16)] * 2,
            DMA, DMA, *[DMA((groups,))] * 6,
        ],
        compiler_params=params(collective_id=1),
        name="merge",
    )(iti, *prepared)
    arranged = pltpu.with_memory_space_constraint(arranged, pltpu.VMEM)
    return pl.pallas_call(
        write,
        out_shape=shape((1, 1, 2, groups, rows, 2 * ext), f32),
        in_specs=[VMEM],
        out_specs=ANY,
        scratch_shapes=[DMA((2, groups))],
        name="write",
    )(arranged)


def solution(mesh):
    in_specs = (P("gx", "gy", None, None, None), P("gx", "gy"), P("gx", "gy", None))
    out_specs = P("gx", "gy", None, None, None, None)
    near = 2
    body = functools.partial(on_device, mesh.shape["gx"], mesh.shape["gy"] // near, near)
    return jax.shard_map(body, mesh=mesh, in_specs=in_specs, out_specs=out_specs, check_vma=False)
```

time: 106 us -> 71.8 us (0.68)
  Pallas kernels: 0 us -> 70.9 us
  blocking collectives: 64.2 us -> 0 us
  matrix products: 16.6 us -> 0 us
  waiting for transfers between devices: 9.24 us -> 0 us
  other arithmetic: 5.02 us -> 0 us
  starting transfers between devices: 4.93 us -> 0 us
  local copies, waits for them, and re-layouts: 4.9 us -> 0 us
    pallas_call x0 -> x3, Pallas kernels: none -> 70.9 us  [the longest x1 61.6 us: on_device(): pl.pallas_call(functools.partial(merge, gx_size, ring, near), out_shape=s...]
    all_to_all x1 -> x0, blocking collectives: 64.2 us -> none  [on_device(): lax.all_to_all(sent, 'gy', split_axis=1, concat_axis=1, tiled=True)]
    dot_general x40 -> x0, matrix products: 16.6 us -> none  [the longest x10 4.3 us: cprod(): jnp.dot(left[0], right[1], precision=highest, preferred_element_type=jnp....]
    ppermute x1 -> x0, waiting for transfers between devices: 9.24 us -> none  [from_partner(): lax.ppermute(x, axis, [(i, i ^ 1 << bit) for i in range(lax.axis_size(axi...]
    ppermute x1 -> x0, starting transfers between devices: 4.93 us -> none  [from_partner(): lax.ppermute(x, axis, [(i, i ^ 1 << bit) for i in range(lax.axis_size(axi...]
    select_n x4 -> x0, other arithmetic: 3.48 us -> none  [the longest x2 1.96 us: on_device(): sent = jnp.take(split, inverse, axis=1)]
    gather x1 -> x0, local copies, waits for them, and re-layouts: 2.1 us -> none  [on_device(): sent = jnp.take(split, inverse, axis=1)]
    broadcast_in_dim x1 -> x0, local copies, waits for them, and re-layouts: 1.56 us -> none  [on_device(): return received[None, None]]
  transfers between devices with their start and end apart: 1 -> 0, of which waited for: 1 -> 0; matrix products, arithmetic and copies ran while one was open for 2% -> 0% of each run, Pallas kernels for 0% -> 0%
where the time goes in v2:
time: 71.8 us; the launch traced here: 71.6 us
  Pallas kernels  70.9 us (99%)
    pallas_call x1, Pallas kernels, on_device(): pl.pallas_call(functools.partial(merge, gx_size, ring, near), out_shape=s...  61.6 us
    pallas_call x1, Pallas kernels, on_device(): pl.pallas_call(functools.partial(prepare, gx_size, ring, near), out_shape...  7.71 us
    pallas_call x1, Pallas kernels, on_device(): pl.pallas_call(write, out_shape=shape((1, 1, 2, groups, rows, 2 * ext), f...  1.67 us

profile of v2, /device:TPU:448, one launch (start us, length us, event | category | flops | bytes accessed | tf_op | source)
XLA Modules:
  0.0 71.6 jit_solution(1291262135268708062)
XLA Ops:
  0.7 7.7 %prepare.1 = (f32[2,128,128]{2,1,0:T(8,128)S(1)}, bf16[256,256]{1,0:T(8,128)(2,1)S(1)}, bf16[256,256]{1,0:T(8,128)(2,1)S(1)}, bf16[256,768]{1,0:T(8,128)(2,1)S(1...) custom-call(s32[1,1,16]{2,1,0:T(1,128)} %owner.1, ...), custom_call_target="tpu_custom_call" | custom-call | tf_op jit(solution)/shard_map/prepare/pallas_call | solution.py:226
  8.4 61.6 %merge.1.arranged = f32[2,16,24,768]{3,2,1,0:T(8,128)S(1)} custom-call(f32[1,1,2,512,512]{4,3,2,1,0:T(8,128)} %iti.3, f32[2,128,128]{2,1,0:T(8,128)S(1)} %get-tuple-element.14.qss, bf16[256,256]{1,0:T(8,128)(2,1)S(1)} %get-tuple-element.15.edge_high, bf16[256,256]{1,0:T(8,128)(2,1)S(1)} %get-tuple-element.16.edge_low, ...), custom_call_target="tpu_custom_call" | custom-call | tf_op jit(solution)/shard_map/merge/pallas_call | solution.py:246
  69.9 1.7 %write.1 = f32[1,1,2,16,24,768]{5,4,3,2,1,0:T(8,128)} custom-call(f32[2,16,24,768]{3,2,1,0:T(8,128)S(1)} %merge.1.arranged), custom_call_target="tpu_custom_call" | custom-call | tf_op jit(solution)/shard_map/write/pallas_call | solution.py:262

commit v3 on v2

v3 whole, which is shorter than its diff:
```python
import functools
import math

import jax
import jax.numpy as jnp
from jax import lax
from jax.experimental import pallas as pl
from jax.experimental.pallas import tpu as pltpu
from jax.sharding import PartitionSpec as P

SWEEPS = 15
LEVELS = (SWEEPS + 1).bit_length() - 1
MESH = pl.DeviceIdType.MESH
EARLY, LATE = (2, 1, 0), (3,)
f32, bf16 = jnp.float32, jnp.bfloat16
VMEM, HBM, SMEM = (pl.BlockSpec(memory_space=m) for m in (pltpu.VMEM, pltpu.HBM, pltpu.SMEM))
DMA = pltpu.SemaphoreType.DMA


def split(x):
    high = x.astype(bf16)
    return high, (x - high.astype(f32)).astype(bf16)


def right_form(x):
    n = x.shape[1] // 2
    return jnp.concatenate([x, jnp.concatenate([-x[:, n:], x[:, :n]], axis=1)], axis=0)


def product(left, right):
    dot = functools.partial(jnp.dot, preferred_element_type=f32)
    return dot(left[0], right[0]) + (dot(left[0], right[1]) + dot(left[1], right[0]))


def both(x):
    high, low = split(x)
    return right_form(high), right_form(low)


def layout(ring, near):
    gy = lax.axis_index("gy")
    y, x = gy // near, lax.rem(gy, near)

    def index(s, t):
        return lax.rem(y + s + ring, ring) * near + lax.rem(x + t + near, near)

    half = ring // 2
    ahead = [(s, t) for s in range(1, half) for t in range(near)] + [(half, 0)]
    behind = [(-s, t) for s in range(1, half) for t in range(near)] + [(-half, 1)]
    places = ahead + [(0, 1)] + behind
    peers = [index(s, t) for s, t in places]
    senders = [index(-s, -t) for s, t in places]
    onward = [index(s - 1, t) for s, t in ahead] + [None] + [index(s + 1, t) for s, t in behind]
    return gy, peers, senders, onward, (index(1, 0), index(-1, 0)), len(ahead)


def sibling_of(gx_size):
    return lax.rem(lax.axis_index("gx") + gx_size // 2, gx_size), lax.axis_index("gy")


def kernel(
    gx_size, ring, near,
    owner, side, iti,
    out,
    owner_s, columns, edge_box, ext_box, left, qss, qse, edge_high, edge_low, ext_high, ext_low, left_high, left_low, base, flag, near_left,
    own_send, other_send, own_in, other_in, flag_in, powers_high, powers_low, solved, solved_in,
    load_sem, send_sem, recv_sem, near_ssem, near_rsem, edge_ssem, edge_rsem, solved_ssem, solved_rsem,
    own_ssem, own_rsem, other_ssem, other_rsem, flag_ssem, flag_rsem,
):
    edge = qss.shape[-1]
    ext = 3 * edge
    groups = ring * near
    rows = ext // groups
    loads = [
        pltpu.make_async_copy(owner, owner_s, load_sem.at[0]),
        pltpu.make_async_copy(iti.at[0, 0, :, :ext, ext:], columns, load_sem.at[1]),
        pltpu.make_async_copy(iti.at[0, 0, :, ext:, :], edge_box, load_sem.at[2]),
        pltpu.make_async_copy(iti.at[0, 0, :, :ext, :ext], ext_box, load_sem.at[3]),
    ]
    for load in loads:
        load.start()
    sibling = sibling_of(gx_size)
    gx = lax.axis_index("gx")
    gy, peers, senders, onward, neighbours, n_ahead = layout(ring, near)
    n_peers = len(peers)
    weight = math.sqrt(edge)
    barrier = pltpu.get_barrier_semaphore()
    pl.semaphore_signal(barrier, inc=1, device_id=sibling, device_id_type=MESH)
    for peer in reversed(peers):
        pl.semaphore_signal(barrier, inc=1, device_id=(gx, peer), device_id_type=MESH)
    pl.semaphore_wait(barrier, n_peers + 1)
    copy = pltpu.make_async_remote_copy(
        iti.at[0, 0, :, ext:, ext:], qss, send_sem, recv_sem, device_id=sibling, device_id_type=MESH
    )
    copy.start()

    loads[0].wait()
    loads[1].wait()
    owners = [owner_s[0, 0, p] for p in range(groups)]
    at = []
    for k, block in enumerate(peers + [gy]):
        panel = jnp.int32(0)
        for p in range(1, groups):
            panel = jnp.maximum(panel, (owners[p] == block).astype(jnp.int32) * p)
        at.append(panel * rows)
        for c in range(2):
            left[k * rows:(k + 1) * rows, c * edge:(c + 1) * edge] = columns[c, pl.ds(at[k], rows), :]
    span = n_ahead * rows
    near_copies = [
        pltpu.make_async_remote_copy(
            left.at[g * ext // 2:g * ext // 2 + span], near_left.at[g], near_ssem.at[g], near_rsem.at[g],
            device_id=(gx, neighbour), device_id_type=MESH,
        )
        for g, neighbour in enumerate(neighbours)
    ]
    for near_copy in near_copies:
        near_copy.start()
    left_high[...], left_low[...] = split(left[...])
    loads[2].wait()
    edge_rows = [edge_box[c] for c in range(2)]
    edge_high[...], edge_low[...] = both(jnp.concatenate([r[:, ext:] for r in edge_rows], axis=1))
    ext_high[...], ext_low[...] = both(jnp.concatenate([r[:, :ext] for r in edge_rows], axis=1))
    flag[...] = jnp.full(flag.shape, side[0, 0].astype(f32))
    loads[3].wait()
    for k in range(groups):
        for c in range(2):
            base[k, c] = ext_box[c, pl.ds(at[k], rows), :] * math.sqrt(edge)
    copy.wait()
    se = pltpu.make_async_remote_copy(
        iti.at[0, 0, :, ext:, :ext], qse, edge_ssem, edge_rsem, device_id=sibling, device_id_type=MESH
    )
    se.start()
    q = split(jnp.concatenate([qss[0], qss[1]], axis=1))
    power = product(q, (edge_high[...], edge_low[...]))
    total = product(q, (ext_high[...], ext_low[...]))
    for level in range(LEVELS):
        high, low = split(power)
        powers_high[level] = high
        powers_low[level] = low
        total = total + product((high, low), both(total))
        if level + 1 < LEVELS:
            power = product((high, low), (right_form(high), right_form(low)))

    def panels(value, buffer, first, add=False):
        for m in range(value.shape[0] // rows):
            for c in range(2):
                piece = value[m * rows:(m + 1) * rows, c * ext:(c + 1) * ext]
                buffer[first + m, c] = base[first + m, c] + piece if add else piece

    def send(k, buffer, into, ssem, rsem, peer):
        copy = pltpu.make_async_remote_copy(
            buffer.at[k], into.at[k], ssem.at[k], rsem.at[k], device_id=(gx, peer), device_id_type=MESH
        )
        copy.start()
        return copy

    own_copies = {}
    factor = both(total)

    pair = [[2 * s, 2 * s + 1, 2 * s + groups // 2, 2 * s + 1 + groups // 2] for s in range(4)]

    def own(s):
        for k in pair[s][::2]:
            at_rows = slice(k * rows, (k + 2) * rows)
            panels(product((left_high[at_rows], left_low[at_rows]), factor) * weight, own_send, k, add=True)

    def send_own(s):
        for k in (pair[s][0], pair[s][2], pair[s][1], pair[s][3]):
            if k < n_peers:
                own_copies[k] = send(k, own_send, own_in, own_ssem, own_rsem, peers[k])

    for s in EARLY:
        own(s)
        send_own(s)
    for s in LATE:
        own(s)
    flags = [
        pltpu.make_async_remote_copy(
            flag, flag_in.at[k], flag_ssem.at[k], flag_rsem.at[k], device_id=(gx, peer), device_id_type=MESH
        )
        for k, peer in enumerate(peers)
    ]
    se.wait()
    total = jnp.concatenate([qse[0], qse[1]], axis=1)
    for level in range(LEVELS):
        total = total + product((powers_high[level], powers_low[level]), both(total))
    solved[...] = total
    solved_copies = [
        pltpu.make_async_remote_copy(
            solved, solved_in.at[g], solved_ssem.at[g], solved_rsem.at[g], device_id=(gx, neighbour), device_id_type=MESH
        )
        for g, neighbour in enumerate(neighbours)
    ]
    for copy in solved_copies:
        copy.start()
    for s in LATE:
        send_own(s)
    for copy in flags:
        copy.start()
    other_copies = {}
    for k in (n_ahead, n_peers):
        at_rows = slice((k // 2) * 2 * rows, (k // 2) * 2 * rows + 2 * rows)
        value = product((left_high[at_rows], left_low[at_rows]), both(total)) * weight
        panels(value[(k % 2) * rows:(k % 2 + 1) * rows], other_send, k)
        if k < n_peers:
            other_copies[k] = send(k, other_send, other_in, other_ssem, other_rsem, peers[k])
    for g in range(2):
        first = g * groups // 2
        near_copies[g].wait()
        solved_copies[g].wait()
        value = product(split(near_left[g]), both(solved_in[g])) * weight
        panels(value[:rows], other_in, first)
        panels(value[rows:], other_send, first + 1)
        for k in reversed(range(first + 1, first + n_ahead)):
            other_copies[k] = send(k, other_send, other_in, other_ssem, other_rsem, onward[k])

    def arrange(own_part, other_part, east, sender):
        for c in range(2):
            east_rows = jnp.broadcast_to(east[:1, :1], (rows, ext)) == 1
            a, b = own_part[c], other_part[c]
            out[c, sender, :, :ext] = jnp.where(east_rows, b, a)
            out[c, sender, :, ext:] = jnp.where(east_rows, a, b)

    arrange(own_send.at[n_peers], other_send.at[n_peers], flag[...], gy)
    for k in range(n_peers):
        flags[k].wait()
        own_copies[k].wait()
        if k in other_copies:
            other_copies[k].wait()
        arrange(own_in.at[k], other_in.at[k], flag_in[k], senders[k])


def on_device(gx_size, ring, near, iti, side, owner):
    width = iti.shape[-1]
    edge = width // 4
    ext = 3 * edge
    groups = ring * near
    rows = ext // groups
    span = (groups - near) // 2 * rows
    vmem, sems = pltpu.VMEM, DMA((groups,))
    iti, owner = (pltpu.with_memory_space_constraint(a, pltpu.HBM) for a in (iti, owner))
    out = pl.pallas_call(
        functools.partial(kernel, gx_size, ring, near),
        out_shape=jax.ShapeDtypeStruct((2, groups, rows, 2 * ext), f32),
        in_specs=[HBM, SMEM, HBM],
        out_specs=VMEM,
        scratch_shapes=[
            pltpu.SMEM((1, 1, groups), jnp.int32), vmem((2, ext, edge), f32), vmem((2, edge, width), f32),
            vmem((2, ext, ext), f32), vmem((ext, 2 * edge), f32),
            vmem((2, edge, edge), f32), vmem((2, edge, ext), f32),
            *[vmem((2 * edge, 2 * edge), bf16)] * 2, *[vmem((2 * edge, 2 * ext), bf16)] * 2,
            *[vmem((ext, 2 * edge), bf16)] * 2, vmem((groups, 2, rows, ext), f32), vmem((1, 128), f32),
            vmem((2, span, 2 * edge), f32),
            *[vmem((groups, 2, rows, ext), f32)] * 4, vmem((groups, 1, 128), f32),
            *[vmem((LEVELS, edge, 2 * edge), bf16)] * 2, vmem((edge, 2 * ext), f32), vmem((2, edge, 2 * ext), f32),
            DMA((4,)), DMA, DMA, DMA((2,)), DMA((2,)), DMA, DMA, DMA((2,)), DMA((2,)), *[sems] * 6,
        ],
        compiler_params=pltpu.CompilerParams(
            collective_id=0, has_side_effects=True, vmem_limit_bytes=40 * 2**20
        ),
        name="merge",
    )(owner, side, iti)
    return out[None, None]


def solution(mesh):
    in_specs = (P("gx", "gy", None, None, None), P("gx", "gy"), P("gx", "gy", None))
    out_specs = P("gx", "gy", None, None, None, None)
    near = 2
    body = functools.partial(on_device, mesh.shape["gx"], mesh.shape["gy"] // near, near)
    return jax.shard_map(body, mesh=mesh, in_specs=in_specs, out_specs=out_specs, check_vma=False)
```

time: 71.8 us -> 70.2 us (0.978); the launches traced: 71.6 us -> 69.2 us
  Pallas kernels: 70.9 us -> 67.1 us
  local copies, waits for them, and re-layouts: 0 us -> 1.41 us
    pallas_call x3 -> x1, Pallas kernels: 70.9 us -> 67.1 us  [on_device(): pl.pallas_call(functools.partial(kernel, gx_size, ring, near), out_shape=...]
    unnamed x0 -> x1, local copies, waits for them, and re-layouts: none -> 1.41 us
where the time goes in v3:
time: 70.2 us; the launch traced here: 69.2 us
  Pallas kernels  67.1 us (96%)
  local copies, waits for them, and re-layouts  1.41 us (2%)
    pallas_call x1, Pallas kernels, on_device(): pl.pallas_call(functools.partial(kernel, gx_size, ring, near), out_shape=...  67.1 us
    unnamed x1, local copies, waits for them, and re-layouts  1.41 us

profile of v3, /device:TPU:448, one launch (start us, length us, event | category | flops | bytes accessed | tf_op | source)
XLA Modules:
  0.0 69.2 jit_solution(11133385981607768301)
XLA Ops:
  0.7 67.1 %merge.1 = f32[2,16,24,768]{3,2,1,0:T(8,128)S(1)} custom-call(s32[1,1,16]{2,1,0:T(1,128)} %owner.1, s32[1,1]{1,0:T(1,128)S(6)} %copy.5.side, f32[1,1,2,512,512]{4,3,2,1,0:T(8,128)} %iti.1), custom_call_target="tpu_custom_call" | custom-call | tf_op jit(solution)/shard_map/merge/pallas_call | solution.py:242
  67.8 1.4 %copy.6 = f32[1,1,2,16,24,768]{5,4,3,2,1,0:T(8,128)} copy(f32[1,1,2,16,24,768]{5,4,3,2,1,0:T(8,128)S(1)} %bitcast.1) | data formatting | bytes 4718592

commit v4 on v3

--- a/solution.py
+++ b/solution.py
@@ -11,7 +11,7 @@
 SWEEPS = 15
 LEVELS = (SWEEPS + 1).bit_length() - 1
 MESH = pl.DeviceIdType.MESH
-EARLY, LATE = (2, 1, 0), (3,)
+EARLY, LATE = (2, 1), (0, 3)
 f32, bf16 = jnp.float32, jnp.bfloat16
 VMEM, HBM, SMEM = (pl.BlockSpec(memory_space=m) for m in (pltpu.VMEM, pltpu.HBM, pltpu.SMEM))
 DMA = pltpu.SemaphoreType.DMA
@@ -62,7 +62,7 @@
     gx_size, ring, near,
     owner, side, iti,
     out,
-    owner_s, columns, edge_box, ext_box, left, qss, qse, edge_high, edge_low, ext_high, ext_low, left_high, left_low, base, flag, near_left,
+    owner_s, columns, edge_box, ext_box, left, qss, qse, edge_high, edge_low, ext_high, ext_low, left_high, left_low, flag, near_left,
     own_send, other_send, own_in, other_in, flag_in, powers_high, powers_low, solved, solved_in,
     load_sem, send_sem, recv_sem, near_ssem, near_rsem, edge_ssem, edge_rsem, solved_ssem, solved_rsem,
     own_ssem, own_rsem, other_ssem, other_rsem, flag_ssem, flag_rsem,
@@ -121,10 +121,6 @@
     edge_high[...], edge_low[...] = both(jnp.concatenate([r[:, ext:] for r in edge_rows], axis=1))
     ext_high[...], ext_low[...] = both(jnp.concatenate([r[:, :ext] for r in edge_rows], axis=1))
     flag[...] = jnp.full(flag.shape, side[0, 0].astype(f32))
-    loads[3].wait()
-    for k in range(groups):
-        for c in range(2):
-            base[k, c] = ext_box[c, pl.ds(at[k], rows), :] * math.sqrt(edge)
     copy.wait()
     se = pltpu.make_async_remote_copy(
         iti.at[0, 0, :, ext:, :ext], qse, edge_ssem, edge_rsem, device_id=sibling, device_id_type=MESH
@@ -145,7 +141,9 @@
         for m in range(value.shape[0] // rows):
             for c in range(2):
                 piece = value[m * rows:(m + 1) * rows, c * ext:(c + 1) * ext]
-                buffer[first + m, c] = base[first + m, c] + piece if add else piece
+                if add:
+                    piece = ext_box[c, pl.ds(at[first + m], rows), :] * weight + piece
+                buffer[first + m, c] = piece
 
     def send(k, buffer, into, ssem, rsem, peer):
         copy = pltpu.make_async_remote_copy(
@@ -169,6 +167,7 @@
             if k < n_peers:
                 own_copies[k] = send(k, own_send, own_in, own_ssem, own_rsem, peers[k])
 
+    loads[3].wait()
     for s in EARLY:
         own(s)
         send_own(s)
@@ -249,7 +248,7 @@
             vmem((2, ext, ext), f32), vmem((ext, 2 * edge), f32),
             vmem((2, edge, edge), f32), vmem((2, edge, ext), f32),
             *[vmem((2 * edge, 2 * edge), bf16)] * 2, *[vmem((2 * edge, 2 * ext), bf16)] * 2,
-            *[vmem((ext, 2 * edge), bf16)] * 2, vmem((groups, 2, rows, ext), f32), vmem((1, 128), f32),
+            *[vmem((ext, 2 * edge), bf16)] * 2, vmem((1, 128), f32),
             vmem((2, span, 2 * edge), f32),
             *[vmem((groups, 2, rows, ext), f32)] * 4, vmem((groups, 1, 128), f32),
             *[vmem((LEVELS, edge, 2 * edge), bf16)] * 2, vmem((edge, 2 * ext), f32), vmem((2, edge, 2 * ext), f32),

time: 70.2 us -> 69.2 us (0.986); the launches traced: 69.2 us -> 69.1 us
  no operation moved by 1% of the time
where the time goes in v4:
time: 69.2 us; the launch traced here: 69.1 us
  Pallas kernels  67 us (97%)
  local copies, waits for them, and re-layouts  1.41 us (2%)
    pallas_call x1, Pallas kernels, on_device(): pl.pallas_call(functools.partial(kernel, gx_size, ring, near), out_shape=...  67 us
    unnamed x1, local copies, waits for them, and re-layouts  1.41 us

profile of v4, /device:TPU:448, one launch (start us, length us, event | category | flops | bytes accessed | tf_op | source)
XLA Modules:
  0.0 69.1 jit_solution(14730887735712328137)
XLA Ops:
  0.7 67.0 %merge.1 = f32[2,16,24,768]{3,2,1,0:T(8,128)S(1)} custom-call(s32[1,1,16]{2,1,0:T(1,128)} %owner.1, s32[1,1]{1,0:T(1,128)S(6)} %copy.5.side, f32[1,1,2,512,512]{4,3,2,1,0:T(8,128)} %iti.1), custom_call_target="tpu_custom_call" | custom-call | tf_op jit(solution)/shard_map/merge/pallas_call | solution.py:241
  67.7 1.4 %copy.6 = f32[1,1,2,16,24,768]{5,4,3,2,1,0:T(8,128)} copy(f32[1,1,2,16,24,768]{5,4,3,2,1,0:T(8,128)S(1)} %bitcast.1) | data formatting | bytes 4718592

commit v5 on v4

--- a/solution.py
+++ b/solution.py
@@ -221,7 +221,10 @@
             out[c, sender, :, ext:] = jnp.where(east_rows, a, b)
 
     arrange(own_send.at[n_peers], other_send.at[n_peers], flag[...], gy)
-    for k in range(n_peers):
+    order = [n_ahead, 0, groups // 2]
+    for g in range(2):
+        order += reversed(range(g * groups // 2 + 1, g * groups // 2 + n_ahead))
+    for k in order:
         flags[k].wait()
         own_copies[k].wait()
         if k in other_copies:

time: 69.2 us -> 68.7 us (level)
  no operation moved by 1% of the time
where the time goes in v5:
time: 68.7 us; the launch traced here: 68.6 us
  Pallas kernels  66.6 us (97%)
  local copies, waits for them, and re-layouts  1.41 us (2%)
    pallas_call x1, Pallas kernels, on_device(): pl.pallas_call(functools.partial(kernel, gx_size, ring, near), out_shape=...  66.6 us
    unnamed x1, local copies, waits for them, and re-layouts  1.41 us

profile of v5, /device:TPU:448, one launch (start us, length us, event | category | flops | bytes accessed | tf_op | source)
XLA Modules:
  0.0 68.6 jit_solution(5925920274941422007)
XLA Ops:
  0.7 66.6 %merge.1 = f32[2,16,24,768]{3,2,1,0:T(8,128)S(1)} custom-call(s32[1,1,16]{2,1,0:T(1,128)} %owner.1, s32[1,1]{1,0:T(1,128)S(6)} %copy.5.side, f32[1,1,2,512,512]{4,3,2,1,0:T(8,128)} %iti.1), custom_call_target="tpu_custom_call" | custom-call | tf_op jit(solution)/shard_map/merge/pallas_call | solution.py:244
  67.2 1.4 %copy.6 = f32[1,1,2,16,24,768]{5,4,3,2,1,0:T(8,128)} copy(f32[1,1,2,16,24,768]{5,4,3,2,1,0:T(8,128)S(1)} %bitcast.1) | data formatting | bytes 4718592
